TPU v7x, 256 devices: a whole 4x4x8 slice. The times are simulated.
256 devices in a mesh: ctx: 128 (over z, y, x_lo, core), head: 2 (over x_hi).
Axes of the slice: x: 4 (x_hi: 2, x_lo: 2; x = x_hi * 2 + x_lo), y: 4, z: 8, core: 2. Of those that a mesh axis runs over, the one named last changes fastest.
Arguments:
- tokens: bfloat16 [65536, 4096], P('ctx', 'head'), may hold values from -3 to 3
- gate_weight: bfloat16 [4096, 32], P('head'), may hold values from -0.04375 to 0.04375
- gate_bias: float32 [32], P('head'), may hold values from 3 to 13
- queries: bfloat16 [65536, 32, 128], P('ctx', 'head'), may hold values from -6.5 to 6.5
- key_vectors: bfloat16 [65536, 32, 128], P('ctx', 'head'), may hold values from -6.5 to 6.5
- values: bfloat16 [65536, 32, 128], P('ctx', 'head'), may hold values from -6 to 6
- pair_table: int32 [128], replicated, may hold values from 0 to 127, each once
Outputs:
- partial_out: float32 [65536, 32, 128], P('ctx', 'head')
- log_total: float32 [65536, 32], P('ctx', 'head')
Inputs may be any that keep to these rules, and one draw needn't show every extreme that they name: Device p holds spans pair_table[p] and 255 - pair_table[p]; every pair once.
All inputs are finite; a program needn't handle non-finite values.
Results may differ from a plain program's by a relative error of at most 0.0025.
Values may be sent and summed in bfloat16 or wider, within the bound.
No kernel may reach another device: no remote copies, remote signals or barrier semaphores. Data moves between devices by JAX's collectives and lax.ppermute only.
A program may use at most 128 MiB of HBM per device.

v0:
```python
import jax
import jax.numpy as jnp
from jax import lax
from jax.sharding import PartitionSpec as P


def passed_along(array, axis, by):
    length = lax.axis_size(axis)
    return lax.ppermute(array, axis, [(i, (i + by) % length) for i in range(length)])


def cumulative(forget, offset, span_len):
    head_count = forget.shape[1]
    log_rows = forget.astype(jnp.float32).reshape(2, span_len, head_count)
    return (offset[:, None, :] + jnp.cumsum(log_rows, axis=1)).reshape(2 * span_len, head_count)


def attend(
    query_block, key_block, value_block, query_rows, key_rows, query_pos, key_pos, score_scale
):
    visible = query_pos[:, None] >= key_pos[None, :]
    products = jnp.einsum(
        "qhd,khd->hqk", query_block, key_block, preferred_element_type=jnp.float32
    )
    scores = products * score_scale + query_rows.T[:, :, None] - key_rows.T[:, None, :]
    row_max = jnp.max(jnp.where(visible[None], scores, -jnp.inf), axis=2)
    weights = jnp.where(visible[None], jnp.exp(scores - row_max[:, :, None]), 0.0)
    denominator = jnp.sum(weights, axis=2)
    weighted = jnp.einsum(
        "hqk,khd->qhd",
        weights.astype(jnp.bfloat16),
        value_block,
        preferred_element_type=jnp.float32,
    )
    return (weighted / denominator.T[:, :, None], (row_max + jnp.log(denominator)).T)


def shards(tokens, gate_weight, gate_bias, queries, key_vectors, values, pair_table):
    tok_rows = queries.shape[0]
    span_len = tok_rows // 2
    head_count = queries.shape[1]
    head_size = queries.shape[2]
    ctx_size = lax.axis_size("ctx")
    device = lax.axis_index("ctx")
    partial_value = jnp.dot(tokens, gate_weight, preferred_element_type=jnp.float32)
    logits = (
        lax.psum_scatter(partial_value, "head", scatter_dimension=1, tiled=True)
        + gate_bias[None, :]
    )
    forget = jax.nn.log_sigmoid(logits).astype(jnp.bfloat16)
    totals = jnp.sum(forget.astype(jnp.float32).reshape(2, span_len, head_count), axis=1)
    every_total = lax.all_gather(totals[None], "ctx", axis=0, tiled=True)
    slot_spans = jnp.stack([pair_table, 2 * ctx_size - 1 - pair_table], axis=1)
    matches = slot_spans[:, :, None] == jnp.arange(2 * ctx_size, dtype=jnp.int32)[None, None, :]
    by_span = jnp.sum(
        jnp.where(matches[:, :, :, None], every_total[:, :, None, :], 0.0), axis=(0, 1)
    )
    running = jnp.cumsum(by_span, axis=0)
    offsets = jnp.concatenate([jnp.zeros((1, head_count), jnp.float32), running[:-1]], axis=0)
    slot_offsets = jnp.sum(
        jnp.where(matches[:, :, :, None], offsets[None, None, :, :], 0.0), axis=2
    )
    nearer = passed_along((key_vectors, values, forget), "ctx", 1)
    farther = passed_along((nearer[0], nearer[1], nearer[2]), "ctx", 1)
    blocks = [(key_vectors, values, forget), nearer, farther]
    within = jnp.arange(span_len, dtype=jnp.int32)
    row_list = []
    pos_list = []
    for distance in range(3):
        source = (device - distance) % ctx_size
        spans = lax.dynamic_index_in_dim(slot_spans, source, 0, keepdims=False)
        offset = lax.dynamic_index_in_dim(slot_offsets, source, 0, keepdims=False)
        row_list.append(cumulative(blocks[distance][2], offset, span_len))
        pos_list.append((spans[:, None] * span_len + within[None, :]).reshape(-1))
    all_keys = jnp.concatenate([blocks[0][0], blocks[1][0], blocks[2][0]], axis=0)
    all_values = jnp.concatenate([blocks[0][1], blocks[1][1], blocks[2][1]], axis=0)
    all_rows = jnp.concatenate(row_list, axis=0)
    all_pos = jnp.concatenate(pos_list, axis=0)
    group_size = 4
    outputs = []
    log_sums = []
    for group_index in range(head_count // group_size):
        lower = group_index * group_size
        upper = lower + group_size
        weighted, log_sum = attend(
            queries[:, lower:upper],
            all_keys[:, lower:upper],
            all_values[:, lower:upper],
            row_list[0][:, lower:upper],
            all_rows[:, lower:upper],
            pos_list[0],
            all_pos,
            head_size ** (-0.5),
        )
        outputs.append(weighted)
        log_sums.append(log_sum)
    return (jnp.concatenate(outputs, axis=1), jnp.concatenate(log_sums, axis=1))


def solution(mesh):
    return jax.shard_map(
        shards,
        mesh=mesh,
        in_specs=(
            P("ctx", "head"),
            P("head", None),
            P("head"),
            P("ctx", "head", None),
            P("ctx", "head", None),
            P("ctx", "head", None),
            P(),
        ),
        out_specs=(P("ctx", "head", None), P("ctx", "head")),
        check_vma=False,
    )
```

profile of v0, /device:TPU:4, one launch (start us, length us, event | category | flops | bytes accessed | tf_op | source)
XLA Modules:
  0.0 360.7 jit_solution(10984810802776107339)
XLA Ops:
  7.2 4.9 %fusion.89 = (bf16[512,16,128]{2,0,1:T(8,128)(2,1)}, bf16[1536,16,128]{2,0,1:T(8,128)(2,1)}) fusion(bf16[512,16,128]{2,1,0:T(8,128)(2,1)} %param.11), kind=kLoop, calls=%fused_computation.137 | loop fusion | bytes 6291456 | tf_op args[4]
  12.2 2.3 fusion.90
  14.5 4.3 %copy.112 = bf16[512,16,128]{0,2,1:T(8,128)(2,1)} copy(bf16[512,16,128]{2,1,0:T(8,128)(2,1)} %param.12) | data formatting | bytes 4194304 | tf_op args[5]
  18.8 1.3 collective-permute-start
  21.1 3.3 fusion.88
  24.7 8.4 %reduce-scatter.2.cloned.1.call-done = f32[512,16]{0,1:T(8,128)} async-done(((f32[512,32]{0,1:T(8,128)}), f32[512,16]{0,1:T(8,128)}) %reduce-scatter.2.cloned.1.call-update) | async-done | bytes 32784 | tf_op jit(solution)/shard_map/reduce_scatter | solution.py:47
  34.2 189.2 %all-gather.1 = f32[128,2,16]{2,1,0:T(2,128)S(1)} all-gather(f32[1,2,16]{2,1,0:T(2,128)S(1)} %bitcast.244), channel_id=2, replica_groups=mesh['ctx'=128,'head'=2] {'ctx'}, dimensions={0}, use_global_device_ids=true | all-gather | bytes 16512 | tf_op jit(solution)/shard_map/all_gather | solution.py:52
  225.2 1.1 reduce-window.30
  227.9 1.2 reduce-window.34
  229.3 28.2 %collective-permute-done.5 = bf16[512,16]{0,1:T(8,128)(2,1)S(1)} collective-permute-done((bf16[512,16]{0,1:T(8,128)(2,1)S(1)}, bf16[512,16]{0,1:T(8,128)(2,1)S(1)}, u32[]{:S(2)}, u32[]{:S(2)}) %collective-permute-start.5) | collective-permute-done | bytes 16416 | tf_op jit(solution)/shard_map/ppermute | solution.py:9
  257.5 1.2 reduce-window.36
  259.4 3.4 constant_dynamic-update-slice_fusion.1
  262.8 3.4 constant_dynamic-update-slice_fusion
  266.2 7.8 %fusion.56 = f32[4,1536,512]{2,1,0:T(8,128)} fusion(bf16[1536,16,128]{2,0,1:T(8,128)(2,1)} %constant_dynamic-update-slice_fusion, bf16[512,4,128]{2,1,0:T(4,128)(2,1)S(1)} %get-tuple-element.27), kind=kOutput, calls=%fused_computation.53 | convolution fusion | flops 805306368 | bytes 19398656 | tf_op jit(solution)/shard_map/qhd,khd->hqk/dot_general | solution.py:22
  274.0 1.8 fusion.58
  275.8 6.3 %fusion.9 = (f32[4,512]{1,0:T(4,128)S(1)}, f32[4,1536,512]{2,1,0:T(8,128)}) fusion(f32[4,1536]{1,0:T(4,128)S(1)} %get-tuple-element.36, f32[4,512]{1,0:T(4,128)S(1)} %get-tuple-element.40, pred[512,1536]{0,1:T(8,128)(4,1)S(1)} %broadcast_compare_fusion, bf16[1536,16,128]{2,0,1:T(8,128)(2,1)S(1)} %bitcast.225, bf16[512,4,128]{2,1,0:T(4,128)(2,1)S(1)} %get-tuple-element.26), kind=kOutput, calls=%fused_computation.17 | convolution fusion | flops 821032960 | bytes 20226048 | tf_op jit(solution)/shard_map/qhd,khd->hqk/dot_general | solution.py:22
  282.1 18.9 %fusion.12 = (f32[4,512]{1,0:T(4,128)S(1)}, f32[4,512]{1,0:T(4,128)S(1)}, f32[4,512]{1,0:T(4,128)S(1)}, f32[4,512]{1,0:T(4,128)S(1)}, f32[4,1536,512]{2,1,0:T(8,128)}) fusion(f32[4,1536,512]{2,1,0:T(8,128)} %get-tuple-element.42, f32[4,512]{1,0:T(4,128)S(1)} %get-tuple-element.41, f32[4,1536]{1,0:T(4,128)S(1)} %get-tuple-element.36, ...), kind=kOutput, calls=%fused_computation.24 | convolution fusion | flops 871358464 | bytes 58105856 | tf_op jit(solution)/shard_map/qhd,khd->hqk/dot_general | solution.py:22
  301.0 15.6 %fusion.14 = (f32[4,512]{1,0:T(4,128)S(1)}, f32[4,512]{1,0:T(4,128)S(1)}, f32[4,512]{1,0:T(4,128)S(1)}) fusion(f32[4,1536,512]{2,1,0:T(8,128)} %get-tuple-element.43, f32[4,512]{1,0:T(4,128)S(1)} %get-tuple-element.13, f32[4,1536]{1,0:T(4,128)S(1)} %get-tuple-element.35, f32[4,512]{1,0:T(4,128)S(1)} %get-tuple-element.39, ...), kind=kLoop, calls=%fused_computation.26 | loop fusion | flops 56616960 | bytes 38682624 | tf_op jit(solution)/shard_map/reduce_sum | solution.py:28
  316.8 9.4 %fusion.44 = f32[512,4,128]{0,2,1:T(8,128)} fusion(f32[4,1536,512]{2,1,0:T(8,128)} %fusion.56, f32[4,512]{1,0:T(4,128)S(1)} %get-tuple-element.15, f32[4,1536]{1,0:T(4,128)S(1)} %get-tuple-element.33, f32[4,512]{1,0:T(4,128)S(1)} %get-tuple-element.37, pred[512,1536]{0,1:T(8,128)(4,1)S(1)} %broadcast_compare_fusion, f32[512,4]{0,1:T(4,128)S(1)} %bitcast.238, ...), kind=kOutput, calls=%fused_computation.49 | convolution fusion | flops 843317248 | bytes 20758528 | tf_op jit(solution)/shard_map/hqk,khd->qhd/dot_general | solution.py:29
  326.2 6.0 %fusion.47 = f32[512,4,128]{0,2,1:T(8,128)} fusion(f32[4,1536,512]{2,1,0:T(8,128)S(1)} %fusion.58, f32[4,512]{1,0:T(4,128)S(1)} %get-tuple-element.14, f32[4,1536]{1,0:T(4,128)S(1)} %get-tuple-element.34, f32[4,512]{1,0:T(4,128)S(1)} %get-tuple-element.38, pred[512,1536]{0,1:T(8,128)(4,1)S(1)} %broadcast_compare_fusion, f32[512,4]{0,1:T(4,128)S(1)} %bitcast.237, ...), kind=kOutput, calls=%fused_computation.50 | convolution fusion | flops 843317248 | bytes 20758528 | tf_op jit(solution)/shard_map/hqk,khd->qhd/dot_general | solution.py:29
  332.2 5.0 %fusion.50 = f32[512,4,128]{0,2,1:T(8,128)S(1)} fusion(f32[4,1536,512]{2,1,0:T(8,128)S(1)} %bitcast.227, f32[4,512]{1,0:T(4,128)S(1)} %get-tuple-element.13, f32[4,1536]{1,0:T(4,128)S(1)} %get-tuple-element.35, f32[4,512]{1,0:T(4,128)S(1)} %get-tuple-element.39, pred[512,1536]{0,1:T(8,128)(4,1)S(1)} %broadcast_compare_fusion, f32[512,4]{0,1:T(4,128)S(1)} %bitcast.236, ...), kind=kOutput, calls=%fused_computation.51 | convolution fusion | flops 843317248 | bytes 20758528 | tf_op jit(solution)/shard_map/hqk,khd->qhd/dot_general | solution.py:29
  337.3 8.0 %fusion.53 = f32[512,4,128]{0,2,1:T(8,128)S(1)} fusion(f32[4,1536,512]{2,1,0:T(8,128)} %get-tuple-element.42, f32[4,512]{1,0:T(4,128)S(1)} %get-tuple-element.41, f32[4,1536]{1,0:T(4,128)S(1)} %get-tuple-element.36, f32[4,512]{1,0:T(4,128)S(1)} %get-tuple-element.40, pred[512,1536]{0,1:T(8,128)(4,1)} %copy-done.2, f32[512,4]{0,1:T(4,128)S(1)} %bitcast.241, ...), kind=kOutput, calls=%fused_computation.52 | convolution fusion | flops 843317248 | bytes 20758528 | tf_op jit(solution)/shard_map/hqk,khd->qhd/dot_general | solution.py:29
  345.3 2.5 pad_maximum_fusion.1
  347.8 5.4 %copy.139 = f32[512,16,128]{2,1,0:T(8,128)} copy(f32[512,16,128]{0,2,1:T(8,128)} %pad_maximum_fusion.1) | data formatting | bytes 8388608
  (97 shorter events, 7.3 us)
Async XLA Ops:
  7.2 5.0 %copy-start = (bf16[512,2048]{1,0:T(8,128)(2,1)S(1)}, bf16[512,2048]{1,0:T(8,128)(2,1)}, u32[]{:S(2)}) copy-start(bf16[512,2048]{1,0:T(8,128)(2,1)} %param.7) | copy-start | bytes 6291460
  7.2 12.9 %copy-start.6 = (s32[128]{0:T(128)S(1)}, s32[128]{0:T(128)}, u32[]{:S(2)}) copy-start(s32[128]{0:T(128)} %param.13) | copy-start | bytes 1540
  7.2 25.9 %copy-start.5 = (f32[16]{0:T(128)S(1)}, f32[16]{0:T(128)}, u32[]{:S(2)}) copy-start(f32[16]{0:T(128)} %param.9) | copy-start | bytes 196
  7.2 25.8 %reduce-scatter.2.cloned.1.call-start = ((), (), s32[]{:S(2)}) async-start(), calls=%async_computation.1 | async-start | bytes 98304 | tf_op jit(solution)/shard_map/reduce_scatter | solution.py:47
  12.2 215.2 %collective-permute-start.2 = (bf16[512,16,128]{2,0,1:T(8,128)(2,1)}, bf16[512,16,128]{2,0,1:T(8,128)(2,1)}, u32[]{:S(2)}, u32[]{:S(2)}) collective-permute-start(bf16[512,16,128]{2,0,1:T(8,128)(2,1)} %get-tuple-element.28), channel_id=1, source_target_pairs={{0,2},{2,4},{4,6},{6,8},{8,10},{10,12},{12,14},{14,16},{16,18},{18... | collective-permute-start | bytes 6291464 | tf_op jit(solution)/shard_map/ppermute | solution.py:9
  18.8 240.3 %collective-permute-start = (bf16[512,16,128]{0,2,1:T(8,128)(2,1)}, bf16[512,16,128]{0,2,1:T(8,128)(2,1)}, u32[]{:S(2)}, u32[]{:S(2)}) collective-permute-start(bf16[512,16,128]{0,2,1:T(8,128)(2,1)} %copy.112), channel_id=1, source_target_pairs={{0,2},{2,4},{4,6},{6,8},{8,10},{10,12},{12,14},{14,16},{16,18},{18... | collective-permute-start | bytes 6291464 | tf_op jit(solution)/shard_map/ppermute | solution.py:9
  21.1 311.1 %copy-start.2 = (pred[512,1536]{0,1:T(8,128)(4,1)}, pred[512,1536]{0,1:T(8,128)(4,1)S(1)}, u32[]{:S(2)}) copy-start(pred[512,1536]{0,1:T(8,128)(4,1)S(1)} %broadcast_compare_fusion) | copy-start | bytes 2359300
  33.9 193.9 %collective-permute-start.4 = (bf16[512,16]{0,1:T(8,128)(2,1)S(1)}, bf16[512,16]{0,1:T(8,128)(2,1)S(1)}, u32[]{:S(2)}, u32[]{:S(2)}) collective-permute-start(bf16[512,16]{0,1:T(8,128)(2,1)S(1)} %get-tuple-element.23), channel_id=1, source_target_pairs={{0,2},{2,4},{4,6},{6,8},{8,10},{10,12},{12,14},{14,16},{16,18},{18... | collective-permute-start | bytes 49160 | tf_op jit(solution)/shard_map/ppermute | solution.py:9
  227.4 35.4 %collective-permute-start.3 = (bf16[512,16,128]{2,0,1:T(8,128)(2,1)}, bf16[512,16,128]{2,0,1:T(8,128)(2,1)}, u32[]{:S(2)}, u32[]{:S(2)}) collective-permute-start(bf16[512,16,128]{2,0,1:T(8,128)(2,1)} %collective-permute-done.2), channel_id=1, source_target_pairs={{0,2},{2,4},{4,6},{6,8},{8,10},{10,12},{12,14},{14,16},{16,18},{18... | collective-permute-start | bytes 6291464 | tf_op jit(solution)/shard_map/ppermute | solution.py:9
  229.1 28.4 %collective-permute-start.5 = (bf16[512,16]{0,1:T(8,128)(2,1)S(1)}, bf16[512,16]{0,1:T(8,128)(2,1)S(1)}, u32[]{:S(2)}, u32[]{:S(2)}) collective-permute-start(bf16[512,16]{0,1:T(8,128)(2,1)S(1)} %collective-permute-done.4), channel_id=1, source_target_pairs={{0,2},{2,4},{4,6},{6,8},{8,10},{10,12},{12,14},{14,16},{16,18},{18... | collective-permute-start | bytes 49160 | tf_op jit(solution)/shard_map/ppermute | solution.py:9
  259.1 57.7 %collective-permute-start.1 = (bf16[512,16,128]{0,2,1:T(8,128)(2,1)}, bf16[512,16,128]{0,2,1:T(8,128)(2,1)S(1)}, u32[]{:S(2)}, u32[]{:S(2)}) collective-permute-start(bf16[512,16,128]{0,2,1:T(8,128)(2,1)} %collective-permute-done), channel_id=1, source_target_pairs={{0,2},{2,4},{4,6},{6,8},{8,10},{10,12},{12,14},{14,16},{16,18},{18... | collective-permute-start | bytes 6291464 | tf_op jit(solution)/shard_map/ppermute | solution.py:9
  266.2 7.8 %slice-start = ((s8[6291456]{0:T(1024)(128)(4,1)}), s8[4194304]{0:T(1024)(128)(4,1)S(1)}, s32[]{:S(2)}) async-start(s8[6291456]{0:T(1024)(128)(4,1)} %bitcast.224), calls=%async_computation.2 | async-start | bytes 8388608
  266.2 7.8 %slice-start.1 = ((s8[6291456]{0:T(1024)(128)(4,1)}), s8[2097152]{0:T(1024)(128)(4,1)S(1)}, s32[]{:S(2)}) async-start(s8[6291456]{0:T(1024)(128)(4,1)} %bitcast.224), calls=%async_computation.3 | async-start | bytes 4194304
  316.7 9.4 %copy-start.7 = (bf16[512,16,128]{0,2,1:T(8,128)(2,1)}, bf16[512,16,128]{0,2,1:T(8,128)(2,1)S(1)}, u32[]{:S(2)}) copy-start(bf16[512,16,128]{0,2,1:T(8,128)(2,1)S(1)} %collective-permute-done.1) | copy-start | bytes 6291460
  316.8 15.4 %slice-start.2 = ((s8[12582912]{0:T(1024)(128)(4,1)}), s8[4194304]{0:T(1024)(128)(4,1)S(1)}, s32[]{:S(2)}) async-start(s8[12582912]{0:T(1024)(128)(4,1)} %bitcast.226), calls=%async_computation.4 | async-start | bytes 8388608
  316.8 15.4 %slice-start.3 = ((s8[12582912]{0:T(1024)(128)(4,1)}), s8[4194304]{0:T(1024)(128)(4,1)S(1)}, s32[]{:S(2)}) async-start(s8[12582912]{0:T(1024)(128)(4,1)} %bitcast.226), calls=%async_computation.5 | async-start | bytes 8388608
  326.2 6.0 %slice-start.4 = ((s8[12582912]{0:T(1024)(128)(4,1)}), s8[4194304]{0:T(1024)(128)(4,1)S(1)}, s32[]{:S(2)}) async-start(s8[12582912]{0:T(1024)(128)(4,1)} %bitcast.226), calls=%async_computation.6 | async-start | bytes 8388608
  332.2 5.1 %copy-start.8 = (bf16[512,16,128]{0,2,1:T(8,128)(2,1)S(1)}, bf16[512,16,128]{0,2,1:T(8,128)(2,1)}, u32[]{:S(2)}) copy-start(bf16[512,16,128]{0,2,1:T(8,128)(2,1)} %copy-done.7) | copy-start | bytes 6291460
  337.3 8.0 %copy-start.3 = (f32[512,4,128]{0,2,1:T(8,128)S(1)}, f32[512,4,128]{0,2,1:T(8,128)}, u32[]{:S(2)}) copy-start(f32[512,4,128]{0,2,1:T(8,128)} %fusion.44) | copy-start | bytes 3145732
  337.3 8.0 %copy-start.4 = (f32[512,4,128]{0,2,1:T(8,128)S(1)}, f32[512,4,128]{0,2,1:T(8,128)}, u32[]{:S(2)}) copy-start(f32[512,4,128]{0,2,1:T(8,128)} %fusion.47) | copy-start | bytes 3145732
  337.3 16.6 %copy-start.1 = (bf16[512,2048]{1,0:T(8,128)(2,1)S(1)}, bf16[512,2048]{1,0:T(8,128)(2,1)}, u32[]{:S(2)}) copy-start(bf16[512,2048]{1,0:T(8,128)(2,1)} %param.7) | copy-start | bytes 6291460
Sparse Core Ops, SparseCore 0:
  14.6 18.4 reduce-scatter.1
where the time goes:
time: 361 us
  blocking collectives  189 us (52%)
  matrix products  65.5 us (18%)
  waiting for transfers between devices  36.6 us (10%)
  other arithmetic  26.9 us (7%)
  local copies, waits for them, and re-layouts  25.9 us (7%)
  between operations  14.5 us (4%)
    all_gather x1, blocking collectives, shards(): every_total = lax.all_gather(totals[None], 'ctx', axis=0, tiled=True)  189 us
    dot_general x4, matrix products, attend(): jnp.einsum('qhd,khd->hqk', query_block, key_block, preferred_element_type...  34.8 us
    dot_general x4, matrix products, attend(): jnp.einsum('hqk,khd->qhd', weights.astype(jnp.bfloat16), value_block, pre...  28.4 us
    ppermute x6, waiting for transfers between devices, passed_along(): lax.ppermute(array, axis, [(i, (i + by) % length) for i in range(length)])  28.2 us
    unnamed x37, local copies, waits for them, and re-layouts  18.2 us
    reduce_sum x1, other arithmetic, attend(): denominator = jnp.sum(weights, axis=2)  15.6 us
    reduce_scatter x1, waiting for transfers between devices, shards(): lax.psum_scatter(partial_value, 'head', scatter_dimension=1, tiled=True)  8.38 us
  transfers between devices with their start and end apart: 7, of which 2 were waited for; matrix products, arithmetic and copies ran while one was open for 21% of the time, Pallas kernels for 0%

commit v1 on v0

v1 whole, which is shorter than its diff:
```python
import functools

import jax
import jax.numpy as jnp
from jax import lax
from jax.experimental import pallas as pl
from jax.experimental.pallas import tpu as pltpu
from jax.sharding import PartitionSpec as P

VMEM_LIMIT = 48 * 1024 * 1024
CHUNK = 4
HALF = 256


def gate_kernel(tok_ref, w_ref, keep_ref, send_ref):
    logits = lax.dot_general(
        w_ref[...], tok_ref[...], (((0,), (1,)), ((), ())), preferred_element_type=jnp.float32
    )
    heads = keep_ref.shape[0]
    first = lax.axis_index("head") == 0
    low, high = logits[:heads], logits[heads:]
    keep_ref[...] = jnp.where(first, low, high)
    send_ref[...] = jnp.where(first, high, low)


def gate_logits(tokens, gate_weight):
    rows, depth = tokens.shape
    heads = gate_weight.shape[1] // 2
    step = 128
    out = jax.ShapeDtypeStruct((heads, rows), jnp.float32)
    return pl.pallas_call(
        gate_kernel,
        grid=(rows // step,),
        in_specs=[
            pl.BlockSpec((step, depth), lambda i: (i, 0)),
            pl.BlockSpec(gate_weight.shape, lambda i: (0, 0)),
        ],
        out_specs=[pl.BlockSpec((heads, step), lambda i: (0, i))] * 2,
        out_shape=[out, out],
        compiler_params=pltpu.CompilerParams(vmem_limit_bytes=VMEM_LIMIT),
        name="gate_logits",
    )(tokens, gate_weight)


def heads_first_kernel(*refs, n_in):
    ins, outs, wide = refs[:n_in], refs[n_in:-1], refs[-1]
    rows, heads, size = ins[0].shape
    for which, ref in enumerate(ins):
        wide[...] = ref[...].reshape(rows * heads, size).astype(jnp.float32)
        for h in range(heads):
            one = wide[pl.ds(h, rows, stride=heads), :].astype(jnp.bfloat16)
            outs[h // CHUNK][h % CHUNK, which] = one


def heads_first(*arrays):
    rows, heads, size = arrays[0].shape
    step = 64
    n_in = len(arrays)
    n_out = heads // CHUNK
    out = jax.ShapeDtypeStruct((CHUNK, n_in, rows, size), jnp.bfloat16)
    return pl.pallas_call(
        functools.partial(heads_first_kernel, n_in=n_in),
        grid=(rows // step,),
        in_specs=[pl.BlockSpec((step, heads, size), lambda i: (i, 0, 0))] * n_in,
        out_specs=[pl.BlockSpec((CHUNK, n_in, step, size), lambda i: (0, 0, i, 0))] * n_out,
        out_shape=[out] * n_out,
        scratch_shapes=[pltpu.VMEM((step * heads, size), jnp.float32)],
        compiler_params=pltpu.CompilerParams(vmem_limit_bytes=VMEM_LIMIT),
        name="heads_first",
    )(*arrays)


def forget_kernel(pair_ref, keep_ref, recv_ref, bias_ref, inner_ref, spread_ref):
    device = lax.axis_index("ctx")
    n_span = 2 * pair_ref.shape[0]
    logits = keep_ref[...] + recv_ref[...] + bias_ref[...]
    forget = (jnp.minimum(logits, 0.0) - jnp.log1p(jnp.exp(-jnp.abs(logits)))).astype(jnp.bfloat16)
    row = lax.broadcasted_iota(jnp.int32, (HALF, HALF), 0)
    col = lax.broadcasted_iota(jnp.int32, (HALF, HALF), 1)
    upto = (row <= col).astype(jnp.float32).astype(jnp.bfloat16)
    low = jnp.dot(forget[:, :HALF], upto, preferred_element_type=jnp.float32)
    high = jnp.dot(forget[:, HALF:], upto, preferred_element_type=jnp.float32)
    inner_ref[:, :HALF] = low
    inner_ref[:, HALF:] = high
    span = pair_ref[device]
    lane = lax.broadcasted_iota(jnp.int32, spread_ref.shape, 1)
    spread_ref[...] = jnp.where(lane == span, low[:, HALF - 1 :], 0.0) + jnp.where(
        lane == n_span - 1 - span, high[:, HALF - 1 :], 0.0
    )


def forget_rows(pair_table, keep, recv, bias):
    heads, rows = keep.shape
    n_span = 2 * pair_table.shape[0]
    whole = pl.BlockSpec(memory_space=pltpu.VMEM)
    return pl.pallas_call(
        forget_kernel,
        in_specs=[pl.BlockSpec(memory_space=pltpu.SMEM), whole, whole, whole],
        out_specs=[whole, whole],
        out_shape=[
            jax.ShapeDtypeStruct((heads, rows), jnp.float32),
            jax.ShapeDtypeStruct((heads, n_span), jnp.float32),
        ],
        compiler_params=pltpu.CompilerParams(vmem_limit_bytes=VMEM_LIMIT),
        name="forget_rows",
    )(pair_table, keep, recv, bias)


def offsets_kernel(pair_ref, by_span_ref, own_ref, near_ref, far_ref, cum_ref):
    n_ctx = pair_ref.shape[0]
    device = lax.axis_index("ctx")
    by_span = by_span_ref[...]
    lane = lax.broadcasted_iota(jnp.int32, by_span.shape, 1)
    for distance, ref in enumerate((own_ref, near_ref, far_ref)):
        span = pair_ref[lax.rem(device + n_ctx - distance, n_ctx)]
        for s, c in enumerate((span, 2 * n_ctx - 1 - span)):
            offset = jnp.sum(jnp.where(lane < c, by_span, 0.0), axis=1, keepdims=True)
            part = slice(s * HALF, (s + 1) * HALF)
            cum_ref[:, distance, part] = ref[:, part] + offset


def offsets(pair_table, by_span, own, near, far):
    heads, rows = own.shape
    whole = pl.BlockSpec(memory_space=pltpu.VMEM)
    return pl.pallas_call(
        offsets_kernel,
        in_specs=[pl.BlockSpec(memory_space=pltpu.SMEM), whole, whole, whole, whole],
        out_specs=whole,
        out_shape=jax.ShapeDtypeStruct((heads, 3, rows), jnp.float32),
        compiler_params=pltpu.CompilerParams(vmem_limit_bytes=VMEM_LIMIT),
        name="offsets",
    )(pair_table, by_span, own, near, far)


def attend_kernel(pair_ref, q_ref, own_ref, near_ref, far_ref, cum_ref, *rest, scale, sub):
    out_ref, log_ref = rest[-2:]
    flat = out_ref.reshape(out_ref.shape[0] * out_ref.shape[2], out_ref.shape[3])
    n_ctx = pair_ref.shape[0]
    device = lax.axis_index("ctx")
    span = pair_ref[device]
    near_lower = span > pair_ref[lax.rem(device + n_ctx - 1, n_ctx)]
    far_lower = span > pair_ref[lax.rem(device + n_ctx - 2, n_ctx)]
    if len(rest) > 2:
        out_ref[...] = rest[0][...]
    row = lax.broadcasted_iota(jnp.int32, (HALF, HALF), 0)
    col = lax.broadcasted_iota(jnp.int32, (HALF, HALF), 1)
    tri = row >= col
    sources = (own_ref, near_ref, far_ref)

    def one_half(h, s, pieces):
        q = q_ref[h, 0, s * HALF : (s + 1) * HALF, :]
        scores = []
        for source, half, masked in pieces:
            part = slice(half * HALF, (half + 1) * HALF)
            prod = lax.dot_general(
                q, sources[source][h, 0, part, :], (((1,), (1,)), ((), ())),
                preferred_element_type=jnp.float32,
            )
            sc = prod * scale - cum_ref[h, source : source + 1, part]
            scores.append(jnp.where(tri, sc, -jnp.inf) if masked else sc)
        top = functools.reduce(jnp.maximum, scores)
        top = jnp.max(top, axis=1, keepdims=True)
        total = None
        acc = None
        for sc, (source, half, _) in zip(scores, pieces):
            part = slice(half * HALF, (half + 1) * HALF)
            w = jnp.exp(sc - top)
            total = w if total is None else total + w
            o = jnp.dot(
                w.astype(jnp.bfloat16), sources[source][h, 1, part, :],
                preferred_element_type=jnp.float32,
            )
            acc = o if acc is None else acc + o
        total = jnp.sum(total, axis=1, keepdims=True)
        flat[pl.ds(s * HALF * 8 + sub + h, HALF, stride=8), :] = acc / total
        log_ref[h, s * HALF : (s + 1) * HALF, :] = top + jnp.log(total)

    for near_is in (False, True):
        for far_is in (False, True):
            lower = [(0, 0, True)]
            upper = [(0, 0, False), (0, 1, True), (1, 0, False), (2, 0, False)]
            (lower if near_is else upper).append((1, 0 if near_is else 1, False))
            (lower if far_is else upper).append((2, 0 if far_is else 1, False))

            @pl.when((near_lower == near_is) & (far_lower == far_is))
            def _(lower=lower, upper=upper):
                @pl.loop(0, q_ref.shape[0])
                def _(h):
                    one_half(h, 0, lower)
                    one_half(h, 1, upper)


def attend(index, pair_table, q, own, near, far, cum, previous):
    heads, _, rows = cum.shape
    size = q.shape[-1]
    group = index * CHUNK // 8
    sub = index * CHUNK % 8
    whole = pl.BlockSpec(own.shape, lambda i: (0, 0, 0, 0))
    block = pl.BlockSpec((rows, 1, 8, size), lambda i: (0, group, 0, 0))
    out = jax.ShapeDtypeStruct((rows, heads // 8, 8, size), jnp.float32)
    in_specs = [
        pl.BlockSpec(memory_space=pltpu.SMEM),
        pl.BlockSpec(q.shape, lambda i: (0, 0, 0, 0)),
        whole,
        whole,
        whole,
        pl.BlockSpec((CHUNK, 3, rows), lambda i: (index, 0, 0)),
    ]
    args = [pair_table, q, own, near, far, cum]
    aliases = {}
    if previous is not None:
        in_specs.append(block if sub else pl.BlockSpec(memory_space=pl.ANY))
        args.append(previous)
        aliases = {6: 0}
    kernel = attend_kernel
    return pl.pallas_call(
        functools.partial(kernel, scale=size**-0.5, sub=sub) if sub or previous is None
        else functools.partial(skip_previous, scale=size**-0.5, sub=sub),
        grid=(1,),
        in_specs=in_specs,
        out_specs=[block, pl.BlockSpec((CHUNK, rows, 1), lambda i: (0, 0, 0))],
        out_shape=[out, jax.ShapeDtypeStruct((CHUNK, rows, 1), jnp.float32)],
        input_output_aliases=aliases,
        compiler_params=pltpu.CompilerParams(vmem_limit_bytes=VMEM_LIMIT),
        name="attend",
    )(*args)


def skip_previous(*refs, scale, sub):
    attend_kernel(*refs[:6], *refs[7:], scale=scale, sub=sub)


def shards(tokens, gate_weight, gate_bias, queries, key_vectors, values, pair_table):
    rows, heads, size = queries.shape
    n_ctx = lax.axis_size("ctx")
    even = lax.rem(lax.axis_index("ctx"), 2) == 0
    all_pairs = [(i, (i + 1) % n_ctx) for i in range(n_ctx)]
    two_pairs = [(i, (i + 2) % n_ctx) for i in range(n_ctx)]
    even_two = [(i, (i + 2) % n_ctx) for i in range(0, n_ctx, 2)]
    even_one = [(i, i + 1) for i in range(0, n_ctx, 2)]

    keep, send = gate_logits(tokens, gate_weight)
    recv = lax.ppermute(send, "head", [(0, 1), (1, 0)])
    own = heads_first(key_vectors, values)
    inner, spread = forget_rows(pair_table, keep, recv, gate_bias[:, None])
    n_chunk = heads // CHUNK
    near = [None] * n_chunk
    direct = [None] * n_chunk
    near[0] = lax.ppermute(own[0], "ctx", all_pairs)
    direct[0] = lax.ppermute(own[0], "ctx", even_two)
    by_span = spread
    by_span = by_span + lax.ppermute(by_span, "ctx", [(i, i ^ 2) for i in range(n_ctx)])
    near_inner = lax.ppermute(inner, "ctx", all_pairs)
    far_inner = lax.ppermute(inner, "ctx", two_pairs)
    later, by_span, near_inner, far_inner = lax.optimization_barrier(
        (own[1:], by_span, near_inner, far_inner)
    )
    own = [own[0], *later]
    for c in range(1, n_chunk):
        near[c] = lax.ppermute(own[c], "ctx", all_pairs)
        direct[c] = lax.ppermute(own[c], "ctx", even_two)
    for bit in (1, 4, 8, 16, 32, 64):
        by_span = by_span + lax.ppermute(by_span, "ctx", [(i, i ^ bit) for i in range(n_ctx)])
    cum = offsets(pair_table, by_span, inner, near_inner, far_inner)
    q = heads_first(queries)
    out = None
    logs = []
    for c in range(n_chunk):
        passed = lax.ppermute(near[c], "ctx", even_one)
        far = jnp.where(even, direct[c], passed)
        out, log = attend(c, pair_table, q[c], own[c], near[c], far, cum, out)
        logs.append(log[:, :, 0])
    log_total = jnp.concatenate(logs, axis=0).T + cum[:, 0, :].T
    return out.reshape(rows, heads, size), log_total


def solution(mesh):
    return jax.shard_map(
        shards,
        mesh=mesh,
        in_specs=(
            P("ctx", "head"),
            P("head", None),
            P("head"),
            P("ctx", "head", None),
            P("ctx", "head", None),
            P("ctx", "head", None),
            P(),
        ),
        out_specs=(P("ctx", "head", None), P("ctx", "head")),
        check_vma=False,
    )
```

time: 361 us -> 181 us (0.50)
  the two profiles are of different devices: /device:TPU:4 before, /device:TPU:18 now
where the time goes in v1:
time: 181 us
  waiting for transfers between devices  62.9 us (35%)
  starting transfers between devices  57.1 us (32%)
  Pallas kernels  42.7 us (24%)
  other arithmetic  10 us (6%)
  local copies, waits for them, and re-layouts  6.95 us (4%)
    pallas_call x4, Pallas kernels, attend(): pl.pallas_call(functools.partial(kernel, scale=size ** (-0.5), sub=sub) i...  30.8 us
    ppermute x3, starting transfers between devices, shards(): direct[c] = lax.ppermute(own[c], 'ctx', even_two)  25.2 us
    ppermute x1, waiting for transfers between devices, shards(): recv = lax.ppermute(send, 'head', [(0, 1), (1, 0)])  20.6 us
    ppermute x3, waiting for transfers between devices, shards(): direct[c] = lax.ppermute(own[c], 'ctx', even_two)  18.8 us
    ppermute x6, waiting for transfers between devices, shards(): lax.ppermute(by_span, 'ctx', [(i, i ^ bit) for i in range(n_ctx)])  13.6 us
    ppermute x6, starting transfers between devices, shards(): lax.ppermute(by_span, 'ctx', [(i, i ^ bit) for i in range(n_ctx)])  11.4 us
    pallas_call x2, Pallas kernels, heads_first(): pl.pallas_call(functools.partial(heads_first_kernel, n_in=n_in), grid=(ro...  9.04 us
    ppermute x4, starting transfers between devices, shards(): passed = lax.ppermute(near[c], 'ctx', even_one)  8.94 us
  transfers between devices with their start and end apart: 22, of which 9 were waited for; matrix products, arithmetic and copies ran while one was open for 3% of the time, Pallas kernels for 7%

profile of v1, /device:TPU:18, one launch (start us, length us, event | category | flops | bytes accessed | tf_op | source)
XLA Modules:
  0.0 180.7 jit_solution(13858224376757179862)
XLA Ops:
  0.7 7.3 %heads_first.3 = (bf16[4,2,512,128]{3,2,1,0:T(8,128)(2,1)}, bf16[4,2,512,128]{3,2,1,0:T(8,128)(2,1)S(1)}, bf16[4,2,512,128]{3,2,1,0:T(8,128)(2,1)S(1)}, bf16[4,2,512,128]{3,2,1,0:T(8,128)(2,1)S(1)}) custom-call(bf16[512,16,128]{2,1,0:T(8,128)(2,1)} %refs_0_.4, bf16[512,16,128]{2,1,0:T(8,128)(2,1)} %refs_1_.1), custom_call_target="tpu_custom_call" | custom-call | tf_op jit(solution)/shard_map/heads_first/pallas_call | solution.py:61
  10.9 3.2 %collective-permute-start.20 = (bf16[4,2,512,128]{3,2,1,0:T(8,128)(2,1)}, bf16[4,2,512,128]{3,2,1,0:T(8,128)(2,1)}, u32[]{:S(2)}, u32[]{:S(2)}) collective-permute-start(bf16[4,2,512,128]{3,2,1,0:T(8,128)(2,1)} %get-tuple-element.45.own_ref), channel_id=1, source_target_pairs={{0,4},{4,8},{8,12},{12,16},{16,20},{20,24},{24,28},{28,32},{32,36}... | collective-permute-start | bytes 3145736 | tf_op jit(solution)/shard_map/ppermute | solution.py:250
  15.8 2.5 %collective-permute-start = (f32[16,512]{1,0:T(8,128)S(1)}, f32[16,512]{1,0:T(8,128)S(1)}, u32[]{:S(2)}, u32[]{:S(2)}) collective-permute-start(f32[16,512]{1,0:T(8,128)S(1)} %get-tuple-element.33), channel_id=1, source_target_pairs={{0,1},{1,0},{2,3},{3,2},{4,5},{5,4},{6,7},{7,6},{8,9},{9,8},{10,11... | collective-permute-start | bytes 98312 | tf_op jit(solution)/shard_map/ppermute | solution.py:243
  18.4 20.6 %collective-permute-done.recv_ref = f32[16,512]{1,0:T(8,128)S(1)} collective-permute-done((f32[16,512]{1,0:T(8,128)S(1)}, f32[16,512]{1,0:T(8,128)S(1)}, u32[]{:S(2)}, u32[]{:S(2)}) %collective-permute-start) | collective-permute-done | bytes 32800 | tf_op jit(solution)/shard_map/ppermute | solution.py:243
  41.9 3.5 %collective-permute-done.1 = f32[16,256]{1,0:T(8,128)S(1)} collective-permute-done((f32[16,256]{1,0:T(8,128)S(1)}, f32[16,256]{1,0:T(8,128)S(1)}, u32[]{:S(2)}, u32[]{:S(2)}) %collective-permute-start.1) | collective-permute-done | bytes 16416 | tf_op jit(solution)/shard_map/ppermute | solution.py:252
  45.5 3.1 %collective-permute-start.16 = (bf16[4,2,512,128]{3,2,1,0:T(8,128)(2,1)}, bf16[4,2,512,128]{3,2,1,0:T(8,128)(2,1)S(1)}, u32[]{:S(2)}, u32[]{:S(2)}) collective-permute-start(bf16[4,2,512,128]{3,2,1,0:T(8,128)(2,1)} %copy-done.6), channel_id=1, source_target_pairs={{0,2},{2,4},{4,6},{6,8},{8,10},{10,12},{12,14},{14,16},{16,18},{18... | collective-permute-start | bytes 3145736 | tf_op jit(solution)/shard_map/ppermute | solution.py:260
  52.6 2.2 %collective-permute-done.8 = f32[16,256]{1,0:T(8,128)S(1)} collective-permute-done((f32[16,256]{1,0:T(8,128)S(1)}, f32[16,256]{1,0:T(8,128)S(1)}, u32[]{:S(2)}, u32[]{:S(2)}) %collective-permute-start.8) | collective-permute-done | bytes 16416 | tf_op jit(solution)/shard_map/ppermute | solution.py:263
  54.8 5.2 %collective-permute-done.9 = f32[16,256]{1,0:T(8,128)S(1)} collective-permute-done((f32[16,256]{1,0:T(8,128)S(1)}, f32[16,256]{1,0:T(8,128)S(1)}, u32[]{:S(2)}, u32[]{:S(2)}) %collective-permute-start.9) | collective-permute-done | bytes 16416 | tf_op jit(solution)/shard_map/ppermute | solution.py:263
  60.1 3.6 %collective-permute-done.10 = f32[16,256]{1,0:T(8,128)S(1)} collective-permute-done((f32[16,256]{1,0:T(8,128)S(1)}, f32[16,256]{1,0:T(8,128)S(1)}, u32[]{:S(2)}, u32[]{:S(2)}) %collective-permute-start.10) | collective-permute-done | bytes 16416 | tf_op jit(solution)/shard_map/ppermute | solution.py:263
  63.7 3.8 %collective-permute-start.11 = (f32[16,256]{1,0:T(8,128)S(1)}, f32[16,256]{1,0:T(8,128)S(1)}, u32[]{:S(2)}, u32[]{:S(2)}) collective-permute-start(f32[16,256]{1,0:T(8,128)S(1)} %add.31), channel_id=1, source_target_pairs={{0,64},{2,66},{4,68},{6,70},{8,72},{10,74},{12,76},{14,78},{16,80}... | collective-permute-start | bytes 49160 | tf_op jit(solution)/shard_map/ppermute | solution.py:263
  69.3 4.3 %collective-permute-start.12 = (f32[16,256]{1,0:T(8,128)S(1)}, f32[16,256]{1,0:T(8,128)S(1)}, u32[]{:S(2)}, u32[]{:S(2)}) collective-permute-start(f32[16,256]{1,0:T(8,128)S(1)} %add.32), channel_id=1, source_target_pairs={{0,128},{2,130},{4,132},{6,134},{8,136},{10,138},{12,140},{14,142}... | collective-permute-start | bytes 49160 | tf_op jit(solution)/shard_map/ppermute | solution.py:263
  73.5 12.9 %collective-permute-start.17 = (bf16[4,2,512,128]{3,2,1,0:T(8,128)(2,1)}, bf16[4,2,512,128]{3,2,1,0:T(8,128)(2,1)S(1)}, u32[]{:S(2)}, u32[]{:S(2)}) collective-permute-start(bf16[4,2,512,128]{3,2,1,0:T(8,128)(2,1)} %copy-done.6), channel_id=1, source_target_pairs={{0,4},{4,8},{8,12},{12,16},{16,20},{20,24},{24,28},{28,32},{32,36}... | collective-permute-start | bytes 3145736 | tf_op jit(solution)/shard_map/ppermute | solution.py:261
  87.2 2.0 %collective-permute-start.21 = (bf16[4,2,512,128]{3,2,1,0:T(8,128)(2,1)}, bf16[4,2,512,128]{3,2,1,0:T(8,128)(2,1)S(1)}, u32[]{:S(2)}, u32[]{:S(2)}) collective-permute-start(bf16[4,2,512,128]{3,2,1,0:T(8,128)(2,1)} %collective-permute-done.19.near_ref), channel_id=1, source_target_pairs={{0,2},{4,6},{8,10},{12,14},{16,18},{20,22},{24,26},{28,30},{32,34}... | collective-permute-start | bytes 3145736 | tf_op jit(solution)/shard_map/ppermute | solution.py:269
  89.2 2.3 %collective-permute-start.18 = (bf16[4,2,512,128]{3,2,1,0:T(8,128)(2,1)S(1)}, bf16[4,2,512,128]{3,2,1,0:T(8,128)(2,1)}, u32[]{:S(2)}, u32[]{:S(2)}) collective-permute-start(bf16[4,2,512,128]{3,2,1,0:T(8,128)(2,1)S(1)} %collective-permute-done.16.near_ref), channel_id=1, source_target_pairs={{0,2},{4,6},{8,10},{12,14},{16,18},{20,22},{24,26},{28,30},{32,34}... | collective-permute-start | bytes 3145736 | tf_op jit(solution)/shard_map/ppermute | solution.py:269
  91.5 18.8 %collective-permute-done.17 = bf16[4,2,512,128]{3,2,1,0:T(8,128)(2,1)S(1)} collective-permute-done((bf16[4,2,512,128]{3,2,1,0:T(8,128)(2,1)}, bf16[4,2,512,128]{3,2,1,0:T(8,128)(2,1)S(1)}, u32[]{:S(2)}, u32[]{:S(2)}) %collective-permute-start.17) | collective-permute-done | bytes 1048608 | tf_op jit(solution)/shard_map/ppermute | solution.py:261
  110.3 5.2 %collective-permute-start.14 = (bf16[4,2,512,128]{3,2,1,0:T(8,128)(2,1)}, bf16[4,2,512,128]{3,2,1,0:T(8,128)(2,1)}, u32[]{:S(2)}, u32[]{:S(2)}) collective-permute-start(bf16[4,2,512,128]{3,2,1,0:T(8,128)(2,1)} %copy-done.4), channel_id=1, source_target_pairs={{0,4},{4,8},{8,12},{12,16},{16,20},{20,24},{24,28},{28,32},{32,36}... | collective-permute-start | bytes 3145736 | tf_op jit(solution)/shard_map/ppermute | solution.py:261
  115.5 2.4 %collective-permute-start.15 = (bf16[4,2,512,128]{3,2,1,0:T(8,128)(2,1)S(1)}, bf16[4,2,512,128]{3,2,1,0:T(8,128)(2,1)}, u32[]{:S(2)}, u32[]{:S(2)}) collective-permute-start(bf16[4,2,512,128]{3,2,1,0:T(8,128)(2,1)S(1)} %collective-permute-done.13.refs_3_), channel_id=1, source_target_pairs={{0,2},{4,6},{8,10},{12,14},{16,18},{20,22},{24,26},{28,30},{32,34}... | collective-permute-start | bytes 3145736 | tf_op jit(solution)/shard_map/ppermute | solution.py:269
  117.9 6.4 %collective-permute-done.4.near_ref = bf16[4,2,512,128]{3,2,1,0:T(8,128)(2,1)S(1)} collective-permute-done((bf16[4,2,512,128]{3,2,1,0:T(8,128)(2,1)}, bf16[4,2,512,128]{3,2,1,0:T(8,128)(2,1)S(1)}, u32[]{:S(2)}, u32[]{:S(2)}) %collective-permute-start.4) | collective-permute-done | bytes 1048608 | tf_op jit(solution)/shard_map/ppermute | solution.py:260
  124.3 7.1 %collective-permute-start.5 = (bf16[4,2,512,128]{3,2,1,0:T(8,128)(2,1)}, bf16[4,2,512,128]{3,2,1,0:T(8,128)(2,1)}, u32[]{:S(2)}, u32[]{:S(2)}) collective-permute-start(bf16[4,2,512,128]{3,2,1,0:T(8,128)(2,1)} %copy-done.2), channel_id=1, source_target_pairs={{0,4},{4,8},{8,12},{12,16},{16,20},{20,24},{24,28},{28,32},{32,36}... | collective-permute-start | bytes 3145736 | tf_op jit(solution)/shard_map/ppermute | solution.py:261
  132.4 2.3 %collective-permute-start.6 = (bf16[4,2,512,128]{3,2,1,0:T(8,128)(2,1)S(1)}, bf16[4,2,512,128]{3,2,1,0:T(8,128)(2,1)}, u32[]{:S(2)}, u32[]{:S(2)}) collective-permute-start(bf16[4,2,512,128]{3,2,1,0:T(8,128)(2,1)S(1)} %collective-permute-done.4.near_ref), channel_id=1, source_target_pairs={{0,2},{4,6},{8,10},{12,14},{16,18},{20,22},{24,26},{28,30},{32,34}... | collective-permute-start | bytes 3145736 | tf_op jit(solution)/shard_map/ppermute | solution.py:269
  140.1 7.8 %attend.4 = (f32[512,2,8,128]{3,2,1,0:T(8,128)}, f32[4,512,1]{2,1,0:T(8,128)S(1)}) custom-call(s32[128]{0:T(128)S(1)} %copy-done.18, bf16[4,1,512,128]{3,2,1,0:T(8,128)(2,1)S(1)} %get-tuple-element.44.q_ref, bf16[4,2,512,128]{3,2,1,0:T(8,128)(2,1)} %get-tuple-element.45.own_ref, bf16[4,2,512,128]{3,2,1,0:T(8,128)(2,1)} %collective-permute-done.19.near_ref, ...), custom_call_target="tpu_custom_call" | custom-call | tf_op jit(solution)/shard_map/attend/pallas_call | solution.py:216
  154.8 7.9 %attend.5 = (f32[512,2,8,128]{3,2,1,0:T(8,128)}, f32[4,512,1]{2,1,0:T(8,128)S(1)}) custom-call(s32[128]{0:T(128)S(1)} %copy-done.18, bf16[4,1,512,128]{3,2,1,0:T(8,128)(2,1)S(1)} %copy-done.17, bf16[4,2,512,128]{3,2,1,0:T(8,128)(2,1)S(1)} %copy-done.7, ...), custom_call_target="tpu_custom_call", output_to_operand_aliasing={{0}: (6, {})} | custom-call | tf_op jit(solution)/shard_map/attend/pallas_call | solution.py:216
  162.7 6.9 %attend.6 = (f32[512,2,8,128]{3,2,1,0:T(8,128)}, f32[4,512,1]{2,1,0:T(8,128)S(1)}) custom-call(s32[128]{0:T(128)S(1)} %copy-done.18, bf16[4,1,512,128]{3,2,1,0:T(8,128)(2,1)S(1)} %copy-done.15, bf16[4,2,512,128]{3,2,1,0:T(8,128)(2,1)S(1)} %copy-done.5, bf16[4,2,512,128]{3,2,1,0:T(8,128)(2,1)S(1)} %collective-permute-done.13.refs_3_, ...), custom_call_target="tpu_custom_call", output_to_operand_aliasing={{0}: (6, {})} | custom-call | tf_op jit(solution)/shard_map/attend/pallas_call | solution.py:216
  169.6 8.2 %attend.7 = (f32[512,2,8,128]{3,2,1,0:T(8,128)}, f32[4,512,1]{2,1,0:T(8,128)S(1)}) custom-call(s32[128]{0:T(128)S(1)} %copy-done.18, bf16[4,1,512,128]{3,2,1,0:T(8,128)(2,1)S(1)} %copy-done.13, bf16[4,2,512,128]{3,2,1,0:T(8,128)(2,1)S(1)} %copy-done.3, bf16[4,2,512,128]{3,2,1,0:T(8,128)(2,1)S(1)} %collective-permute-done.4.near_ref, ...), custom_call_target="tpu_custom_call", output_to_operand_aliasing={{0}: (6, {})} | custom-call | tf_op jit(solution)/shard_map/attend/pallas_call | solution.py:216
  (94 shorter events, 30.2 us)
Async XLA Ops:
  0.7 38.3 %copy-start.18 = (s32[128]{0:T(128)S(1)}, s32[128]{0:T(128)}, u32[]{:S(2)}) copy-start(s32[128]{0:T(128)} %pair_ref.9) | copy-start | bytes 1540
  10.9 75.6 %collective-permute-start.19 = (bf16[4,2,512,128]{3,2,1,0:T(8,128)(2,1)}, bf16[4,2,512,128]{3,2,1,0:T(8,128)(2,1)}, u32[]{:S(2)}, u32[]{:S(2)}) collective-permute-start(bf16[4,2,512,128]{3,2,1,0:T(8,128)(2,1)} %get-tuple-element.45.own_ref), channel_id=1, source_target_pairs={{0,2},{2,4},{4,6},{6,8},{8,10},{10,12},{12,14},{14,16},{16,18},{18... | collective-permute-start | bytes 3145736 | tf_op jit(solution)/shard_map/ppermute | solution.py:249
  10.9 76.3 %collective-permute-start.20 = (bf16[4,2,512,128]{3,2,1,0:T(8,128)(2,1)}, bf16[4,2,512,128]{3,2,1,0:T(8,128)(2,1)}, u32[]{:S(2)}, u32[]{:S(2)}) collective-permute-start(bf16[4,2,512,128]{3,2,1,0:T(8,128)(2,1)} %get-tuple-element.45.own_ref), channel_id=1, source_target_pairs={{0,4},{4,8},{8,12},{12,16},{16,20},{20,24},{24,28},{28,32},{32,36}... | collective-permute-start | bytes 3145736 | tf_op jit(solution)/shard_map/ppermute | solution.py:250
  15.8 23.2 %collective-permute-start = (f32[16,512]{1,0:T(8,128)S(1)}, f32[16,512]{1,0:T(8,128)S(1)}, u32[]{:S(2)}, u32[]{:S(2)}) collective-permute-start(f32[16,512]{1,0:T(8,128)S(1)} %get-tuple-element.33), channel_id=1, source_target_pairs={{0,1},{1,0},{2,3},{3,2},{4,5},{5,4},{6,7},{7,6},{8,9},{9,8},{10,11... | collective-permute-start | bytes 98312 | tf_op jit(solution)/shard_map/ppermute | solution.py:243
  39.8 5.7 %collective-permute-start.2 = (f32[16,512]{1,0:T(8,128)S(1)}, f32[16,512]{1,0:T(8,128)S(1)}, u32[]{:S(2)}, u32[]{:S(2)}) collective-permute-start(f32[16,512]{1,0:T(8,128)S(1)} %get-tuple-element.35.own_ref), channel_id=1, source_target_pairs={{0,2},{2,4},{4,6},{6,8},{8,10},{10,12},{12,14},{14,16},{16,18},{18... | collective-permute-start | bytes 98312 | tf_op jit(solution)/shard_map/ppermute | solution.py:253
  39.8 5.6 %collective-permute-start.3 = (f32[16,512]{1,0:T(8,128)S(1)}, f32[16,512]{1,0:T(8,128)S(1)}, u32[]{:S(2)}, u32[]{:S(2)}) collective-permute-start(f32[16,512]{1,0:T(8,128)S(1)} %get-tuple-element.35.own_ref), channel_id=1, source_target_pairs={{0,4},{2,6},{4,8},{6,10},{8,12},{10,14},{12,16},{14,18},{16,20},{1... | collective-permute-start | bytes 98312 | tf_op jit(solution)/shard_map/ppermute | solution.py:254
  41.7 3.7 %collective-permute-start.1 = (f32[16,256]{1,0:T(8,128)S(1)}, f32[16,256]{1,0:T(8,128)S(1)}, u32[]{:S(2)}, u32[]{:S(2)}) collective-permute-start(f32[16,256]{1,0:T(8,128)S(1)} %get-tuple-element.34), channel_id=1, source_target_pairs={{0,4},{2,6},{4,0},{6,2},{8,12},{10,14},{12,8},{14,10},{16,20},{18,... | collective-permute-start | bytes 49160 | tf_op jit(solution)/shard_map/ppermute | solution.py:252
  45.5 43.7 %collective-permute-start.16 = (bf16[4,2,512,128]{3,2,1,0:T(8,128)(2,1)}, bf16[4,2,512,128]{3,2,1,0:T(8,128)(2,1)S(1)}, u32[]{:S(2)}, u32[]{:S(2)}) collective-permute-start(bf16[4,2,512,128]{3,2,1,0:T(8,128)(2,1)} %copy-done.6), channel_id=1, source_target_pairs={{0,2},{2,4},{4,6},{6,8},{8,10},{10,12},{12,14},{14,16},{16,18},{18... | collective-permute-start | bytes 3145736 | tf_op jit(solution)/shard_map/ppermute | solution.py:260
  48.5 2.5 %collective-permute-start.7 = (f32[16,256]{1,0:T(8,128)S(1)}, f32[16,256]{1,0:T(8,128)S(1)}, u32[]{:S(2)}, u32[]{:S(2)}) collective-permute-start(f32[16,256]{1,0:T(8,128)S(1)} %add.27), channel_id=1, source_target_pairs={{0,2},{2,0},{4,6},{6,4},{8,10},{10,8},{12,14},{14,12},{16,18},{18,... | collective-permute-start | bytes 49160 | tf_op jit(solution)/shard_map/ppermute | solution.py:263
  51.0 3.7 %collective-permute-start.8 = (f32[16,256]{1,0:T(8,128)S(1)}, f32[16,256]{1,0:T(8,128)S(1)}, u32[]{:S(2)}, u32[]{:S(2)}) collective-permute-start(f32[16,256]{1,0:T(8,128)S(1)} %add.28), channel_id=1, source_target_pairs={{0,8},{2,10},{4,12},{6,14},{8,0},{10,2},{12,4},{14,6},{16,24},{18,... | collective-permute-start | bytes 49160 | tf_op jit(solution)/shard_map/ppermute | solution.py:263
  54.8 5.2 %collective-permute-start.9 = (f32[16,256]{1,0:T(8,128)S(1)}, f32[16,256]{1,0:T(8,128)S(1)}, u32[]{:S(2)}, u32[]{:S(2)}) collective-permute-start(f32[16,256]{1,0:T(8,128)S(1)} %add.29), channel_id=1, source_target_pairs={{0,16},{2,18},{4,20},{6,22},{8,24},{10,26},{12,28},{14,30},{16,0},... | collective-permute-start | bytes 49160 | tf_op jit(solution)/shard_map/ppermute | solution.py:263
  60.0 3.7 %collective-permute-start.10 = (f32[16,256]{1,0:T(8,128)S(1)}, f32[16,256]{1,0:T(8,128)S(1)}, u32[]{:S(2)}, u32[]{:S(2)}) collective-permute-start(f32[16,256]{1,0:T(8,128)S(1)} %add.30), channel_id=1, source_target_pairs={{0,32},{2,34},{4,36},{6,38},{8,40},{10,42},{12,44},{14,46},{16,48}... | collective-permute-start | bytes 49160 | tf_op jit(solution)/shard_map/ppermute | solution.py:263
  63.7 5.5 %collective-permute-start.11 = (f32[16,256]{1,0:T(8,128)S(1)}, f32[16,256]{1,0:T(8,128)S(1)}, u32[]{:S(2)}, u32[]{:S(2)}) collective-permute-start(f32[16,256]{1,0:T(8,128)S(1)} %add.31), channel_id=1, source_target_pairs={{0,64},{2,66},{4,68},{6,70},{8,72},{10,74},{12,76},{14,78},{16,80}... | collective-permute-start | bytes 49160 | tf_op jit(solution)/shard_map/ppermute | solution.py:263
  69.3 17.2 %collective-permute-start.12 = (f32[16,256]{1,0:T(8,128)S(1)}, f32[16,256]{1,0:T(8,128)S(1)}, u32[]{:S(2)}, u32[]{:S(2)}) collective-permute-start(f32[16,256]{1,0:T(8,128)S(1)} %add.32), channel_id=1, source_target_pairs={{0,128},{2,130},{4,132},{6,134},{8,136},{10,138},{12,140},{14,142}... | collective-permute-start | bytes 49160 | tf_op jit(solution)/shard_map/ppermute | solution.py:263
  73.5 36.7 %collective-permute-start.17 = (bf16[4,2,512,128]{3,2,1,0:T(8,128)(2,1)}, bf16[4,2,512,128]{3,2,1,0:T(8,128)(2,1)S(1)}, u32[]{:S(2)}, u32[]{:S(2)}) collective-permute-start(bf16[4,2,512,128]{3,2,1,0:T(8,128)(2,1)} %copy-done.6), channel_id=1, source_target_pairs={{0,4},{4,8},{8,12},{12,16},{16,20},{20,24},{24,28},{28,32},{32,36}... | collective-permute-start | bytes 3145736 | tf_op jit(solution)/shard_map/ppermute | solution.py:261
  86.5 29.0 %collective-permute-start.13 = (bf16[4,2,512,128]{3,2,1,0:T(8,128)(2,1)}, bf16[4,2,512,128]{3,2,1,0:T(8,128)(2,1)S(1)}, u32[]{:S(2)}, u32[]{:S(2)}) collective-permute-start(bf16[4,2,512,128]{3,2,1,0:T(8,128)(2,1)} %copy-done.4), channel_id=1, source_target_pairs={{0,2},{2,4},{4,6},{6,8},{8,10},{10,12},{12,14},{14,16},{16,18},{18... | collective-permute-start | bytes 3145736 | tf_op jit(solution)/shard_map/ppermute | solution.py:260
  86.6 37.7 %collective-permute-start.4 = (bf16[4,2,512,128]{3,2,1,0:T(8,128)(2,1)}, bf16[4,2,512,128]{3,2,1,0:T(8,128)(2,1)S(1)}, u32[]{:S(2)}, u32[]{:S(2)}) collective-permute-start(bf16[4,2,512,128]{3,2,1,0:T(8,128)(2,1)} %copy-done.2), channel_id=1, source_target_pairs={{0,2},{2,4},{4,6},{6,8},{8,10},{10,12},{12,14},{14,16},{16,18},{18... | collective-permute-start | bytes 3145736 | tf_op jit(solution)/shard_map/ppermute | solution.py:260
  87.2 44.2 %collective-permute-start.21 = (bf16[4,2,512,128]{3,2,1,0:T(8,128)(2,1)}, bf16[4,2,512,128]{3,2,1,0:T(8,128)(2,1)S(1)}, u32[]{:S(2)}, u32[]{:S(2)}) collective-permute-start(bf16[4,2,512,128]{3,2,1,0:T(8,128)(2,1)} %collective-permute-done.19.near_ref), channel_id=1, source_target_pairs={{0,2},{4,6},{8,10},{12,14},{16,18},{20,22},{24,26},{28,30},{32,34}... | collective-permute-start | bytes 3145736 | tf_op jit(solution)/shard_map/ppermute | solution.py:269
  89.2 61.3 %collective-permute-start.18 = (bf16[4,2,512,128]{3,2,1,0:T(8,128)(2,1)S(1)}, bf16[4,2,512,128]{3,2,1,0:T(8,128)(2,1)}, u32[]{:S(2)}, u32[]{:S(2)}) collective-permute-start(bf16[4,2,512,128]{3,2,1,0:T(8,128)(2,1)S(1)} %collective-permute-done.16.near_ref), channel_id=1, source_target_pairs={{0,2},{4,6},{8,10},{12,14},{16,18},{20,22},{24,26},{28,30},{32,34}... | collective-permute-start | bytes 3145736 | tf_op jit(solution)/shard_map/ppermute | solution.py:269
  110.3 21.1 %copy-start.19 = (bf16[4,2,512,128]{3,2,1,0:T(8,128)(2,1)}, bf16[4,2,512,128]{3,2,1,0:T(8,128)(2,1)S(1)}, u32[]{:S(2)}) copy-start(bf16[4,2,512,128]{3,2,1,0:T(8,128)(2,1)S(1)} %collective-permute-done.17) | copy-start | bytes 3145732
  110.3 41.7 %collective-permute-start.14 = (bf16[4,2,512,128]{3,2,1,0:T(8,128)(2,1)}, bf16[4,2,512,128]{3,2,1,0:T(8,128)(2,1)}, u32[]{:S(2)}, u32[]{:S(2)}) collective-permute-start(bf16[4,2,512,128]{3,2,1,0:T(8,128)(2,1)} %copy-done.4), channel_id=1, source_target_pairs={{0,4},{4,8},{8,12},{12,16},{16,20},{20,24},{24,28},{28,32},{32,36}... | collective-permute-start | bytes 3145736 | tf_op jit(solution)/shard_map/ppermute | solution.py:261
  115.5 36.5 %collective-permute-start.15 = (bf16[4,2,512,128]{3,2,1,0:T(8,128)(2,1)S(1)}, bf16[4,2,512,128]{3,2,1,0:T(8,128)(2,1)}, u32[]{:S(2)}, u32[]{:S(2)}) collective-permute-start(bf16[4,2,512,128]{3,2,1,0:T(8,128)(2,1)S(1)} %collective-permute-done.13.refs_3_), channel_id=1, source_target_pairs={{0,2},{4,6},{8,10},{12,14},{16,18},{20,22},{24,26},{28,30},{32,34}... | collective-permute-start | bytes 3145736 | tf_op jit(solution)/shard_map/ppermute | solution.py:269
  124.3 29.1 %collective-permute-start.5 = (bf16[4,2,512,128]{3,2,1,0:T(8,128)(2,1)}, bf16[4,2,512,128]{3,2,1,0:T(8,128)(2,1)}, u32[]{:S(2)}, u32[]{:S(2)}) collective-permute-start(bf16[4,2,512,128]{3,2,1,0:T(8,128)(2,1)} %copy-done.2), channel_id=1, source_target_pairs={{0,4},{4,8},{8,12},{12,16},{16,20},{20,24},{24,28},{28,32},{32,36}... | collective-permute-start | bytes 3145736 | tf_op jit(solution)/shard_map/ppermute | solution.py:261
  132.4 21.0 %collective-permute-start.6 = (bf16[4,2,512,128]{3,2,1,0:T(8,128)(2,1)S(1)}, bf16[4,2,512,128]{3,2,1,0:T(8,128)(2,1)}, u32[]{:S(2)}, u32[]{:S(2)}) collective-permute-start(bf16[4,2,512,128]{3,2,1,0:T(8,128)(2,1)S(1)} %collective-permute-done.4.near_ref), channel_id=1, source_target_pairs={{0,2},{4,6},{8,10},{12,14},{16,18},{20,22},{24,26},{28,30},{32,34}... | collective-permute-start | bytes 3145736 | tf_op jit(solution)/shard_map/ppermute | solution.py:269
  (21 other events, 121.1 us)
